TPU v7x, 32 devices: a whole 2x2x4 slice. The times are simulated.
32 devices in a mesh: segment: 2 (over core), dp: 8 (over z, x), mp: 2 (over y).
Axes of the slice: x: 2, y: 2, z: 4, core: 2. Of those that a mesh axis runs over, the one named last changes fastest.
Arguments:
- grad_top: bfloat16 [4096, 2048], P('dp'), may hold values from -6 to 6
- saved_query: bfloat16 [2, 4096, 2048], P('segment', 'dp', 'mp'), may hold values from -12 to 12
- saved_key: bfloat16 [2, 6144, 2048], P('segment', 'dp', 'mp'), may hold values from -4 to 4
- saved_value: bfloat16 [2, 6144, 2048], P('segment', 'dp', 'mp'), may hold values from -6 to 6
- w_query: bfloat16 [2, 2048, 2048], P('segment', 'mp', 'dp'), may hold values from -0.125 to 0.125
- w_key: bfloat16 [2, 2048, 2048], P('segment', 'mp', 'dp'), may hold values from -0.125 to 0.125
- w_value: bfloat16 [2, 2048, 2048], P('segment', 'mp', 'dp'), may hold values from -0.125 to 0.125
- w_out: bfloat16 [2, 2048, 2048], P('segment', 'mp', 'dp'), may hold values from -0.125 to 0.125
- query_length: int32 [16, 2], P('dp'), may hold values from 64 to 128
- key_offset: int32 [16, 2], P('dp'), may hold values from 0 to 2, as said below
- key_length: int32 [16, 2], P('dp'), may hold values from 64 to 256
- tile_owner: int32 [16, 3], replicated, may hold values from 0 to 47, as said below
Outputs:
- section_grads: bfloat16 [2, 4096, 2048], P('segment', 'dp', 'mp')
- encoder_grads: bfloat16 [6144, 2048], P('dp', ('segment', 'mp'))
Inputs may be any that keep to these rules, and one draw needn't show every extreme that they name: Example 0 takes tiles 0 to key_offset[s, 1] - 1 and example 1 the rest of the sequence's encoder tiles; each example holds at least one tile and its rows fit in its tiles. `tile_owner`: every global tile appears once. Tile t is owned by dp index t // 6; the owner of a tile of dp index i (sequences i * 2 to i * 2 + 1) is i - 1, i or i + 1, wrapping around. Each dp index hands 1 to 2 tiles to each neighbour, and 2 is reached in every draw.
All inputs are finite; a program needn't handle non-finite values.
Results may differ from a plain program's by a relative error of at most 0.019.
Values may be sent and summed in bfloat16 or wider, within the bound.
A program may use at most 128 MiB of HBM per device.

v0:
```python
import jax
import jax.numpy as jnp
from jax import lax
from jax.sharding import PartitionSpec as P

DH = 256
TILE = 128
CAP = 2
masked_floor = -1e30


def shifted(block, axis, distance):
    devices = range(lax.axis_size(axis))
    route = [(i - distance, i) for i in devices if i - distance in devices]
    return lax.ppermute(block, axis, route)


def extended_2(block, sides, width):
    for axis, dim in sides:
        count = lax.axis_size(axis)
        forward = [(i, i + 1) for i in range(count - 1)]
        forward.append((count - 1, 0))
        backward = [(target, source) for source, target in forward]
        low = lax.ppermute(
            lax.slice_in_dim(block, block.shape[dim] - width, None, axis=dim), axis, forward
        )
        high = lax.ppermute(lax.slice_in_dim(block, 0, width, axis=dim), axis, backward)
        block = jnp.concatenate([low, block, high], axis=dim)
    return block


def example_mask(query_length, key_offset, key_length, q_rows, k_rows):
    row_ids = jnp.arange(q_rows, dtype=jnp.int32)[:, None]
    starts = jnp.arange(query_length.shape[0], dtype=jnp.int32)[None, :] * TILE
    inside_q = (row_ids >= starts) & (row_ids < starts + query_length[None, :])
    col_ids = jnp.arange(k_rows, dtype=jnp.int32)[:, None]
    key_start = key_offset[None, :] * TILE
    inside_k = (col_ids >= key_start) & (col_ids < key_start + key_length[None, :])
    return jnp.any(inside_q[:, None, :] & inside_k[None, :, :], axis=-1)


def sequence_backward(operands, query_full, out_full):
    grad_in, query_block, key_block, value_block, query_length, key_offset, key_length = operands
    q_rows, local_width = query_block.shape
    k_rows = key_block.shape[0]
    head_count = local_width // DH
    score_scale = DH ** (-0.5)
    out_grad = lax.dot_general(
        grad_in, out_full, (((1,), (1,)), ((), ())), preferred_element_type=jnp.float32
    ).astype(jnp.bfloat16)
    q_heads = query_block.reshape(q_rows, head_count, DH)
    k_heads = key_block.reshape(k_rows, head_count, DH)
    v_heads = value_block.reshape(k_rows, head_count, DH)
    grad_heads = out_grad.reshape(q_rows, head_count, DH)
    scores = (
        jnp.einsum("qhd,khd->hqk", q_heads, k_heads, preferred_element_type=jnp.float32)
        * score_scale
    )
    allowed = example_mask(query_length, key_offset, key_length, q_rows, k_rows)[None]
    masked = jnp.where(allowed, scores, masked_floor)
    row_max = jnp.max(masked, axis=-1, keepdims=True)
    exp_terms = jnp.where(allowed, jnp.exp(masked - row_max), 0.0)
    denominator = jnp.maximum(jnp.sum(exp_terms, axis=-1, keepdims=True), 1.0)
    attention_probs = exp_terms / denominator
    prob_bf = attention_probs.astype(jnp.bfloat16)
    attended = jnp.einsum("hqk,khd->qhd", prob_bf, v_heads, preferred_element_type=jnp.float32)
    out_dot = jnp.sum(grad_heads.astype(jnp.float32) * attended, axis=-1)
    prob_grad = jnp.einsum("qhd,khd->hqk", grad_heads, v_heads, preferred_element_type=jnp.float32)
    score_grad = (attention_probs * (prob_grad - jnp.transpose(out_dot)[:, :, None])).astype(
        jnp.bfloat16
    )
    query_grad = (
        jnp.einsum("hqk,khd->qhd", score_grad, k_heads, preferred_element_type=jnp.float32)
        * score_scale
    ).astype(jnp.bfloat16)
    key_gradient = (
        jnp.einsum("hqk,qhd->khd", score_grad, q_heads, preferred_element_type=jnp.float32)
        * score_scale
    ).astype(jnp.bfloat16)
    value_grad = jnp.einsum(
        "hqk,qhd->khd", prob_bf, grad_heads, preferred_element_type=jnp.float32
    ).astype(jnp.bfloat16)
    mixed_grad = jnp.dot(
        query_grad.reshape(q_rows, local_width), query_full, preferred_element_type=jnp.float32
    )
    return (
        mixed_grad,
        key_gradient.reshape(k_rows, local_width),
        value_grad.reshape(k_rows, local_width),
    )


def ranked(marked):
    return jnp.cumsum(marked.astype(jnp.int32)) - 1


def on_device(
    grad_top,
    saved_query,
    saved_key,
    saved_value,
    w_query,
    w_key,
    w_value,
    w_out,
    query_length,
    key_offset,
    key_length,
    tile_owner,
):
    segment_count = lax.axis_size("segment")
    segment_id = lax.axis_index("segment")
    micro_count = query_length.shape[0]
    q_rows = grad_top.shape[0] // micro_count
    k_rows = saved_key.shape[1] // micro_count
    width = grad_top.shape[1]
    local_width = saved_query.shape[2]
    half_width = width // lax.axis_size("mp")
    out_full, query_full, key_full, complete_value = (
        lax.all_gather(w_out[0], "dp", axis=1, tiled=True),
        lax.all_gather(w_query[0], "dp", axis=1, tiled=True),
        lax.all_gather(w_key[0], "dp", axis=1, tiled=True),
        lax.all_gather(w_value[0], "dp", axis=1, tiled=True),
    )

    def run_layer(operands):
        return sequence_backward(operands, query_full, out_full)

    def bypass_layer(operands):
        return (
            jnp.zeros((q_rows, width), jnp.float32),
            jnp.zeros((k_rows, local_width), jnp.bfloat16),
            jnp.zeros((k_rows, local_width), jnp.bfloat16),
        )

    incoming = jnp.zeros((q_rows, width), jnp.bfloat16)
    sections = jnp.zeros((micro_count * q_rows, half_width), jnp.bfloat16)
    key_grads = jnp.zeros((micro_count * k_rows, local_width), jnp.bfloat16)
    value_grads = jnp.zeros((micro_count * k_rows, local_width), jnp.bfloat16)
    for clock_tick in range(micro_count + 1):
        step_id = clock_tick - 1 + segment_id
        active = (step_id >= 0) & (step_id < micro_count)
        picked = jnp.clip(step_id, 0, micro_count - 1)
        top_rows = lax.dynamic_slice_in_dim(grad_top, picked * q_rows, q_rows, 0)
        grad_in = jnp.where(segment_id == segment_count - 1, top_rows, incoming)
        query_block = lax.dynamic_slice_in_dim(saved_query[0], picked * q_rows, q_rows, 0)
        key_block = lax.dynamic_slice_in_dim(saved_key[0], picked * k_rows, k_rows, 0)
        value_block = lax.dynamic_slice_in_dim(saved_value[0], picked * k_rows, k_rows, 0)
        lengths_q = lax.dynamic_index_in_dim(query_length, picked, 0, keepdims=False)
        offsets_k = lax.dynamic_index_in_dim(key_offset, picked, 0, keepdims=False)
        lengths_k = lax.dynamic_index_in_dim(key_length, picked, 0, keepdims=False)
        mixed_grad, key_gradient, value_grad = lax.cond(
            active,
            run_layer,
            bypass_layer,
            (grad_in, query_block, key_block, value_block, lengths_q, offsets_k, lengths_k),
        )
        summed_share = lax.psum_scatter(
            mixed_grad.astype(jnp.bfloat16), "mp", scatter_dimension=1, tiled=True
        ).astype(jnp.float32)
        own_input = lax.dynamic_slice_in_dim(
            grad_in, lax.axis_index("mp") * half_width, half_width, 1
        )
        own_section = (own_input.astype(jnp.float32) + summed_share).astype(jnp.bfloat16)
        if clock_tick < micro_count:
            full_section = lax.all_gather(own_section, "mp", axis=1, tiled=True)
        sections = jnp.where(
            active,
            lax.dynamic_update_slice_in_dim(sections, own_section, picked * q_rows, 0),
            sections,
        )
        key_grads = jnp.where(
            active,
            lax.dynamic_update_slice_in_dim(key_grads, key_gradient, picked * k_rows, 0),
            key_grads,
        )
        value_grads = jnp.where(
            active,
            lax.dynamic_update_slice_in_dim(value_grads, value_grad, picked * k_rows, 0),
            value_grads,
        )
        if clock_tick < micro_count:
            incoming = shifted(full_section, "segment", -1)
    encoder_partial = jnp.dot(key_grads, key_full, preferred_element_type=jnp.float32) + jnp.dot(
        value_grads, complete_value, preferred_element_type=jnp.float32
    )
    reduced = lax.psum_scatter(
        encoder_partial.astype(jnp.bfloat16), ("segment", "mp"), scatter_dimension=1, tiled=True
    )
    tiles_dev = reduced.shape[0] // TILE
    features = reduced.shape[1]
    local_tiles = reduced.reshape(tiles_dev, TILE, features)
    devices = lax.axis_size("dp")
    my_index = lax.axis_index("dp")
    owners_all = tile_owner.reshape(devices, tiles_dev)

    def route_plan(source):
        owner_row = lax.dynamic_index_in_dim(owners_all, source % devices, 0, keepdims=False)
        owner_step = (owner_row // tiles_dev - source % devices + devices) % devices
        return (owner_step, owner_row % tiles_dev)

    mine_step, mine_slot = route_plan(my_index)
    left_step, left_slot = route_plan(my_index - 1 + devices)
    right_step, right_slot = route_plan(my_index + 1)
    capacity_ids = jnp.arange(CAP, dtype=jnp.int32)[:, None]
    to_left = mine_step == devices - 1
    rightward_send = mine_step == 1
    pick_left = (ranked(to_left)[None, :] == capacity_ids) & to_left[None, :]
    pick_right = (ranked(rightward_send)[None, :] == capacity_ids) & rightward_send[None, :]
    selector_mask = jnp.concatenate([pick_left, pick_right], axis=0).astype(jnp.bfloat16)
    outgoing = jnp.einsum(
        "sa,ayk->syk", selector_mask, local_tiles, preferred_element_type=jnp.float32
    ).astype(jnp.bfloat16)
    outgoing = outgoing.reshape(2 * CAP * TILE, features)
    extended = extended_2(outgoing, (("dp", 0),), CAP * TILE)
    from_left = extended[: CAP * TILE].reshape(CAP, TILE, features)
    from_right = extended[extended.shape[0] - CAP * TILE :].reshape(CAP, TILE, features)
    candidates = jnp.concatenate([from_left, local_tiles, from_right], axis=0)
    left_marked = left_step == 1
    left_hit = (ranked(left_marked)[None, :] == capacity_ids) & left_marked[None, :]
    left_target = jnp.sum(jnp.where(left_hit, left_slot[None, :], 0), axis=1)
    right_marked = right_step == devices - 1
    right_hit = (ranked(right_marked)[None, :] == capacity_ids) & right_marked[None, :]
    right_target = jnp.sum(jnp.where(right_hit, right_slot[None, :], 0), axis=1)
    target = jnp.concatenate([left_target, mine_slot, right_target])
    usable = jnp.concatenate(
        [jnp.any(left_hit, axis=1), mine_step == 0, jnp.any(right_hit, axis=1)]
    )
    placer = (
        (jnp.arange(tiles_dev, dtype=jnp.int32)[:, None] == target[None, :]) & usable[None, :]
    ).astype(jnp.bfloat16)
    owned_rows = jnp.einsum(
        "sc,crf->srf", placer, candidates, preferred_element_type=jnp.float32
    ).astype(jnp.bfloat16)
    return (sections[None], owned_rows.reshape(tiles_dev * TILE, features))


def solution(mesh):
    in_specs = (
        P("dp", None),
        P("segment", "dp", "mp"),
        P("segment", "dp", "mp"),
        P("segment", "dp", "mp"),
        P("segment", "mp", "dp"),
        P("segment", "mp", "dp"),
        P("segment", "mp", "dp"),
        P("segment", "mp", "dp"),
        P("dp", None),
        P("dp", None),
        P("dp", None),
        P(),
    )
    out_specs = (P("segment", "dp", "mp"), P("dp", ("segment", "mp")))
    return jax.shard_map(
        on_device, mesh=mesh, in_specs=in_specs, out_specs=out_specs, check_vma=False
    )
```

profile of v0, /device:TPU:0, one launch (start us, length us, event | category | flops | bytes accessed | tf_op | source)
XLA Modules:
  0.0 555.0 jit_solution(11707310913632669811)
XLA Ops:
  11.2 76.6 %all-gather.15.cloned.1.call-done = bf16[1,1024,2048]{2,1,0:T(8,128)(2,1)} async-done(((bf16[1,1024,256]{2,1,0:T(8,128)(2,1)}), bf16[1,1024,2048]{2,1,0:T(8,128)(2,1)}) %all-gather.15.cloned.1.call-update) | async-done | bytes 4194320 | tf_op jit(solution)/shard_map/all_gather | solution.py:120
  87.8 75.3 %all-gather.17.cloned.1.call-done = bf16[1,1024,2048]{2,1,0:T(8,128)(2,1)} async-done(((bf16[1,1024,256]{2,1,0:T(8,128)(2,1)}), bf16[1,1024,2048]{2,1,0:T(8,128)(2,1)}) %all-gather.17.cloned.1.call-update) | async-done | bytes 4194320 | tf_op jit(solution)/shard_map/all_gather | solution.py:121
  163.1 3.0 conditional.3
  166.3 46.4 %reduce-scatter.5.cloned.1.call-done = bf16[256,1024]{1,0:T(8,128)(2,1)} async-done(((bf16[256,2048]{1,0:T(8,128)(2,1)}), bf16[256,1024]{1,0:T(8,128)(2,1)}) %reduce-scatter.5.cloned.1.call-update) | async-done | bytes 524304 | tf_op jit(solution)/shard_map/reduce_scatter | solution.py:158
  216.3 21.4 %all-gather.11.cloned.1.call-done = bf16[256,2048]{1,0:T(8,128)(2,1)} async-done(((bf16[256,1024]{1,0:T(8,128)(2,1)}), bf16[256,2048]{1,0:T(8,128)(2,1)}) %all-gather.11.cloned.1.call-update) | async-done | bytes 1048592 | tf_op jit(solution)/shard_map/all_gather | solution.py:166
  239.4 3.1 collective-permute-done
  242.6 3.0 dynamic-slice_select_fusion.1
  245.5 31.3 %conditional.4 = (bf16[256,2048]{1,0:T(8,128)(2,1)}, bf16[384,1024]{0,1:T(8,128)(2,1)}, bf16[384,1024]{0,1:T(8,128)(2,1)}) conditional(s32[]{:T(128)} %convert_element_type.214, () %tuple.46, (s32[2,2]{1,0:T(2,128)S(1)}, s32[]{:T(128)}, s32[2,2]{1,0:T(2,128)S(1)}, s32[2,2]{1,0:T(2,128)S(1)}, bf16[1,512,1024]{2,1,0:T(8,128)(2,1)}, ...), branch_computations={%region_7.8_spmd, %region_8.13_spmd} | conditional | flops 3363606528 | bytes 75467568 | solution.py:152
  249.0 3.5 constant_dynamic-slice_fusion.6
  257.0 3.4 fusion.94
  260.4 4.6 convolution_convert_fusion.3
  276.9 20.4 %reduce-scatter.7.cloned.1.call-done = bf16[256,1024]{1,0:T(8,128)(2,1)} async-done(((bf16[256,2048]{1,0:T(8,128)(2,1)}), bf16[256,1024]{1,0:T(8,128)(2,1)}) %reduce-scatter.7.cloned.1.call-update) | async-done | bytes 524304 | tf_op jit(solution)/shard_map/reduce_scatter | solution.py:158
  301.5 19.9 %all-gather.13.cloned.1.call-done = bf16[256,2048]{1,0:T(8,128)(2,1)} async-done(((bf16[256,1024]{1,0:T(8,128)(2,1)}), bf16[256,2048]{1,0:T(8,128)(2,1)}) %all-gather.13.cloned.1.call-update) | async-done | bytes 1048592 | tf_op jit(solution)/shard_map/all_gather | solution.py:166
  334.0 23.1 %conditional.5 = (bf16[256,2048]{1,0:T(8,128)(2,1)}, bf16[384,1024]{0,1:T(8,128)(2,1)}, bf16[384,1024]{0,1:T(8,128)(2,1)}) conditional(s32[]{:T(128)} %convert_element_type.219, () %tuple.48, (s32[2,2]{1,0:T(2,128)S(1)}, s32[]{:T(128)}, s32[2,2]{1,0:T(2,128)S(1)}, s32[2,2]{1,0:T(2,128)S(1)}, bf16[1,512,1024]{2,1,0:T(8,128)(2,1)}, ...), branch_computations={%region_14.15_spmd, %region_15.20_spmd} | conditional | flops 3363606528 | bytes 85953360 | solution.py:152
  337.8 3.1 constant_dynamic-slice_fusion.12
  344.1 3.5 convolution_convert_fusion.5
  357.1 3.5 select_dynamic-update-slice_fusion
  360.6 37.9 %all-gather.21.cloned.1.call-done = bf16[1,1024,2048]{2,1,0:T(8,128)(2,1)} async-done(((bf16[1,1024,256]{2,1,0:T(8,128)(2,1)}), bf16[1,1024,2048]{2,1,0:T(8,128)(2,1)}) %all-gather.21.cloned.1.call-update) | async-done | bytes 4194320 | tf_op jit(solution)/shard_map/all_gather | solution.py:123
  398.5 8.8 %fusion.51 = f32[768,2048]{1,0:T(8,128)} fusion(bf16[768,1024]{0,1:T(8,128)(2,1)} %get-tuple-element.478, bf16[1,1024,2048]{2,1,0:T(8,128)(2,1)} %all-gather.21.cloned.1.call-done), kind=kOutput, calls=%fused_computation.106 | convolution fusion | flops 3221225472 | bytes 12058624 | tf_op jit(solution)/shard_map/dot_general | solution.py:184
  407.3 66.5 %all-gather.19.cloned.1.call-done = bf16[1,1024,2048]{2,1,0:T(8,128)(2,1)} async-done(((bf16[1,1024,256]{2,1,0:T(8,128)(2,1)}), bf16[1,1024,2048]{2,1,0:T(8,128)(2,1)}) %all-gather.19.cloned.1.call-update) | async-done | bytes 4194320 | tf_op jit(solution)/shard_map/all_gather | solution.py:122
  473.8 9.6 %add_convert_fusion = bf16[768,2048]{1,0:T(8,128)(2,1)} fusion(f32[768,2048]{1,0:T(8,128)} %fusion.51, bf16[768,1024]{0,1:T(8,128)(2,1)} %get-tuple-element.479, bf16[1,1024,2048]{2,1,0:T(8,128)(2,1)} %all-gather.19.cloned.1.call-done), kind=kOutput, calls=%fused_computation.105 | convolution fusion | flops 3224371200 | bytes 15204352 | tf_op jit(solution)/shard_map/dot_general | solution.py:184
  485.6 34.2 %reduce-scatter.11.cloned.1.call-done = bf16[768,512]{1,0:T(8,128)(2,1)} async-done(((bf16[768,2048]{1,0:T(8,128)(2,1)}), bf16[768,512]{1,0:T(8,128)(2,1)}) %reduce-scatter.11.cloned.1.call-update) | async-done | bytes 786448 | tf_op jit(solution)/shard_map/reduce_scatter | solution.py:187
  524.2 3.3 collective-permute-start.3
  528.8 13.4 %reduce-scatter.9.cloned.1.call-done = bf16[256,1024]{1,0:T(8,128)(2,1)} async-done(((bf16[256,2048]{1,0:T(8,128)(2,1)}), bf16[256,1024]{1,0:T(8,128)(2,1)}) %reduce-scatter.9.cloned.1.call-update) | async-done | bytes 524304 | tf_op jit(solution)/shard_map/reduce_scatter | solution.py:158
  (156 shorter events, 78.4 us)
Async XLA Ops:
  7.2 156.0 %copy-start = (bf16[1,768,1024]{2,1,0:T(8,128)(2,1)S(1)}, bf16[1,768,1024]{2,1,0:T(8,128)(2,1)}, u32[]{:S(2)}) copy-start(bf16[1,768,1024]{2,1,0:T(8,128)(2,1)} %param.20) | copy-start | bytes 4718596
  7.2 156.0 %copy-start.1 = (bf16[1,768,1024]{2,1,0:T(8,128)(2,1)S(1)}, bf16[1,768,1024]{2,1,0:T(8,128)(2,1)}, u32[]{:S(2)}) copy-start(bf16[1,768,1024]{2,1,0:T(8,128)(2,1)} %param.21) | copy-start | bytes 4718596
  7.2 155.9 %copy-start.19 = (s32[2,2]{1,0:T(2,128)S(1)}, s32[2,2]{1,0:T(2,128)}, u32[]{:S(2)}) copy-start(s32[2,2]{1,0:T(2,128)} %param.26) | copy-start | bytes 52
  7.2 155.9 %copy-start.20 = (s32[2,2]{1,0:T(2,128)S(1)}, s32[2,2]{1,0:T(2,128)}, u32[]{:S(2)}) copy-start(s32[2,2]{1,0:T(2,128)} %param.27) | copy-start | bytes 52
  7.2 155.9 %copy-start.21 = (s32[2,2]{1,0:T(2,128)S(1)}, s32[2,2]{1,0:T(2,128)}, u32[]{:S(2)}) copy-start(s32[2,2]{1,0:T(2,128)} %param.28) | copy-start | bytes 52
  7.2 80.6 %all-gather.15.cloned.1.call-start = ((), (), s32[]{:S(2)}) async-start(), calls=%async_computation.10 | async-start | bytes 4718592 | tf_op jit(solution)/shard_map/all_gather | solution.py:120
  7.9 155.2 %all-gather.17.cloned.1.call-start = ((), (), s32[]{:S(2)}) async-start(), calls=%async_computation.11 | async-start | bytes 4718592 | tf_op jit(solution)/shard_map/all_gather | solution.py:121
  8.7 204.0 %reduce-scatter.5.cloned.1.call-start = ((), (), s32[]{:S(2)}) async-start(), calls=%async_computation.4 | async-start | bytes 1572864 | tf_op jit(solution)/shard_map/reduce_scatter | solution.py:158
  166.2 71.5 %all-gather.11.cloned.1.call-start = ((), (), s32[]{:S(2)}) async-start(), calls=%async_computation.5 | async-start | bytes 1572864 | tf_op jit(solution)/shard_map/all_gather | solution.py:166
  216.2 81.1 %reduce-scatter.7.cloned.1.call-start = ((), (), s32[]{:S(2)}) async-start(), calls=%async_computation.6 | async-start | bytes 1572864 | tf_op jit(solution)/shard_map/reduce_scatter | solution.py:158
  237.7 4.9 collective-permute-start
  269.7 3.3 copy-start.24
  276.8 44.6 %all-gather.13.cloned.1.call-start = ((), (), s32[]{:S(2)}) async-start(), calls=%async_computation.7 | async-start | bytes 1572864 | tf_op jit(solution)/shard_map/all_gather | solution.py:166
  300.0 98.5 %all-gather.21.cloned.1.call-start = ((), (), s32[]{:S(2)}) async-start(), calls=%async_computation.13 | async-start | bytes 4718592 | tf_op jit(solution)/shard_map/all_gather | solution.py:123
  300.7 173.1 %all-gather.19.cloned.1.call-start = ((), (), s32[]{:S(2)}) async-start(), calls=%async_computation.12 | async-start | bytes 4718592 | tf_op jit(solution)/shard_map/all_gather | solution.py:122
  301.5 218.3 %reduce-scatter.11.cloned.1.call-start = ((), (), s32[]{:S(2)}) async-start(), calls=%async_computation.9 | async-start | bytes 3932160 | tf_op jit(solution)/shard_map/reduce_scatter | solution.py:187
  321.4 11.2 %collective-permute-start.1 = (bf16[256,2048]{1,0:T(8,128)(2,1)}, bf16[256,2048]{1,0:T(8,128)(2,1)S(1)}, u32[]{:S(2)}, u32[]{:S(2)}) collective-permute-start(bf16[256,2048]{1,0:T(8,128)(2,1)} %all-gather.13.cloned.1.call-done), channel_id=1, source_target_pairs={{16,0},{17,1},{18,2},{19,3},{20,4},{21,5},{22,6},{23,7},{24,8},{25... | collective-permute-start | bytes 3145736 | tf_op jit(solution)/shard_map/ppermute | solution.py:15
  337.8 3.1 copy-start.2
  483.4 58.9 %reduce-scatter.9.cloned.1.call-start = ((), (), s32[]{:S(2)}) async-start(), calls=%async_computation.8 | async-start | bytes 1572864 | tf_op jit(solution)/shard_map/reduce_scatter | solution.py:158
  521.9 20.4 %copy-start.9 = (bf16[256,2048]{1,0:T(8,128)(2,1)S(1)}, bf16[256,2048]{1,0:T(8,128)(2,1)}, u32[]{:S(2)}) copy-start(bf16[256,2048]{1,0:T(8,128)(2,1)} %dynamic-slice_select_fusion) | copy-start | bytes 3145732
  521.9 22.3 %collective-permute-start.2 = (bf16[256,512]{1,0:T(8,128)(2,1)S(1)}, bf16[256,512]{1,0:T(8,128)(2,1)S(1)}, u32[]{:S(2)}, u32[]{:S(2)}) collective-permute-start(bf16[256,512]{1,0:T(8,128)(2,1)S(1)} %bitcast.243), channel_id=1, source_target_pairs={{0,2},{2,4},{4,6},{6,8},{8,10},{10,12},{12,14},{14,0},{1,3},{3,5},... | collective-permute-start | bytes 786440 | tf_op jit(solution)/shard_map/ppermute | solution.py:24
  524.2 20.4 %collective-permute-start.3 = (bf16[256,512]{1,0:T(8,128)(2,1)}, bf16[256,512]{1,0:T(8,128)(2,1)}, u32[]{:S(2)}, u32[]{:S(2)}) collective-permute-start(bf16[256,512]{1,0:T(8,128)(2,1)} %bitcast.70), channel_id=1, source_target_pairs={{2,0},{4,2},{6,4},{8,6},{10,8},{12,10},{14,12},{0,14},{3,1},{5,3},... | collective-permute-start | bytes 786440 | tf_op jit(solution)/shard_map/ppermute | solution.py:27
  528.8 14.9 %copy-start.4 = (bf16[768,512]{1,0:T(8,128)(2,1)S(1)}, bf16[768,512]{1,0:T(8,128)(2,1)}, u32[]{:S(2)}) copy-start(bf16[768,512]{1,0:T(8,128)(2,1)} %reduce-scatter.11.cloned.1.call-done) | copy-start | bytes 2359300
  543.8 3.0 copy-start.13
  (13 other events, 26.0 us)
Sparse Core Ops, SparseCore 0:
  10.1 77.7 all-gather.14
  89.9 73.1 all-gather.16
  166.3 46.3 reduce-scatter.4
  216.3 21.2 all-gather.10
  276.9 20.3 reduce-scatter.6
  300.1 21.2 all-gather.12
  323.5 75.0 all-gather.20
  400.5 73.1 all-gather.18
  483.6 36.1 reduce-scatter.10
  521.9 20.3 reduce-scatter.8
where the time goes:
time: 562 us; the launch traced here: 555 us
  waiting for transfers between devices  418 us (74%)
  matrix products  51.6 us (9%)
  local copies, waits for them, and re-layouts  35.7 us (6%)
  other arithmetic  26.2 us (5%)
  between operations  14.7 us (3%)
  starting transfers between devices  8.2 us (1%)
    reduce_scatter x3, waiting for transfers between devices, on_device(): lax.psum_scatter(mixed_grad.astype(jnp.bfloat16), 'mp', scatter_dimension...  80.3 us
    all_gather x1, waiting for transfers between devices, on_device(): lax.all_gather(w_out[0], 'dp', axis=1, tiled=True)  76.6 us
    all_gather x1, waiting for transfers between devices, on_device(): lax.all_gather(w_query[0], 'dp', axis=1, tiled=True)  75.3 us
    all_gather x1, waiting for transfers between devices, on_device(): lax.all_gather(w_key[0], 'dp', axis=1, tiled=True)  66.5 us
    all_gather x2, waiting for transfers between devices, on_device(): full_section = lax.all_gather(own_section, 'mp', axis=1, tiled=True)  41.3 us
    all_gather x1, waiting for transfers between devices, on_device(): lax.all_gather(w_value[0], 'dp', axis=1, tiled=True)  37.9 us
    reduce_scatter x1, waiting for transfers between devices, on_device(): lax.psum_scatter(encoder_partial.astype(jnp.bfloat16), ('segment', 'mp'),...  34.2 us
    another operation x11, local copies, waits for them, and re-layouts  14.8 us
  transfers between devices with their start and end apart: 14, of which 11 were waited for; matrix products, arithmetic and copies ran while one was open for 10% of the time, Pallas kernels for 0%

commit v1 on v0

--- a/solution.py
+++ b/solution.py
@@ -7,6 +7,28 @@
 TILE = 128
 CAP = 2
 masked_floor = -1e30
+
+
+def joined_along(blocks, dim):
+    lengths = list(blocks.shape[1:])
+    lengths[dim] *= blocks.shape[0]
+    return jnp.moveaxis(blocks, 0, dim).reshape(lengths)
+
+
+def collect(x, axis, dim):
+    size = lax.axis_size(axis)
+    pairs = [(i, (i + 1) % size) for i in range(size)]
+    back = [(b, a) for a, b in pairs]
+    lower, upper = ([], [])
+    for step in range(size - 1):
+        if step % 2 == 0:
+            lower.append(lax.ppermute(lower[-1] if lower else x, axis, pairs))
+        else:
+            upper.append(lax.ppermute(upper[-1] if upper else x, axis, back))
+    blocks = jnp.stack([*lower[::-1], x, *upper])
+    shift = lax.axis_index(axis) - len(lower)
+    blocks = blocks[(jnp.arange(size) - shift) % size]
+    return joined_along(blocks, dim)
 
 
 def shifted(block, axis, distance):
@@ -118,7 +140,7 @@
     half_width = width // lax.axis_size("mp")
     out_full, query_full, key_full, complete_value = (
         lax.all_gather(w_out[0], "dp", axis=1, tiled=True),
-        lax.all_gather(w_query[0], "dp", axis=1, tiled=True),
+        collect(w_query[0], "dp", 1),
         lax.all_gather(w_key[0], "dp", axis=1, tiled=True),
         lax.all_gather(w_value[0], "dp", axis=1, tiled=True),
     )

time: 562 us -> 537 us (0.956)
  waiting for transfers between devices: 418 us -> 357 us
  starting transfers between devices: 8.2 us -> 25.7 us
  local copies, waits for them, and re-layouts: 35.7 us -> 52.7 us
    ppermute x0 -> x7, waiting for transfers between devices: none -> 89.2 us  [the longest x4 87.9 us: collect(): lower.append(lax.ppermute(lower[-1] if lower else x, axis, pairs))]
    all_gather x1 -> x0, waiting for transfers between devices: 75.3 us -> none  [on_device(): lax.all_gather(w_query[0], 'dp', axis=1, tiled=True)]
    all_gather x1, waiting for transfers between devices: 76.6 us -> 2.98 us  [on_device(): lax.all_gather(w_out[0], 'dp', axis=1, tiled=True)]
    ppermute x0 -> x7, starting transfers between devices: none -> 17.6 us  [the longest x3 9.33 us: collect(): upper.append(lax.ppermute(upper[-1] if upper else x, axis, back))]
    unnamed x22 -> x31, local copies, waits for them, and re-layouts: 2.04 us -> 7.94 us
    another operation x11 -> x12, local copies, waits for them, and re-layouts: 14.8 us -> 15.7 us
  transfers between devices with their start and end apart: 14 -> 20, of which waited for: 11 -> 15; matrix products, arithmetic and copies ran while one was open for 10% -> 14% of each run, Pallas kernels for 0% -> 0%
where the time goes in v1:
time: 537 us; the launch traced here: 529 us
  waiting for transfers between devices  357 us (66%)
  local copies, waits for them, and re-layouts  52.7 us (10%)
  matrix products  51.5 us (10%)
  other arithmetic  26.3 us (5%)
  starting transfers between devices  25.7 us (5%)
  between operations  14.4 us (3%)
    ppermute x4, waiting for transfers between devices, collect(): lower.append(lax.ppermute(lower[-1] if lower else x, axis, pairs))  87.9 us
    reduce_scatter x3, waiting for transfers between devices, on_device(): lax.psum_scatter(mixed_grad.astype(jnp.bfloat16), 'mp', scatter_dimension...  80.3 us
    all_gather x1, waiting for transfers between devices, on_device(): lax.all_gather(w_key[0], 'dp', axis=1, tiled=True)  66.5 us
    all_gather x2, waiting for transfers between devices, on_device(): full_section = lax.all_gather(own_section, 'mp', axis=1, tiled=True)  41.5 us
    all_gather x1, waiting for transfers between devices, on_device(): lax.all_gather(w_value[0], 'dp', axis=1, tiled=True)  37.7 us
    reduce_scatter x1, waiting for transfers between devices, on_device(): lax.psum_scatter(encoder_partial.astype(jnp.bfloat16), ('segment', 'mp'),...  34.2 us
    another operation x11, local copies, waits for them, and re-layouts  14.8 us
  transfers between devices with their start and end apart: 20, of which 15 were waited for; matrix products, arithmetic and copies ran while one was open for 14% of the time, Pallas kernels for 0%

profile of v1, /device:TPU:0, one launch (start us, length us, event | category | flops | bytes accessed | tf_op | source)
XLA Modules:
  0.0 528.7 jit_solution(9841933383875597398)
XLA Ops:
  10.9 15.4 %collective-permute-done = bf16[1024,256]{1,0:T(8,128)(2,1)S(1)} collective-permute-done((bf16[1024,256]{1,0:T(8,128)(2,1)}, bf16[1024,256]{1,0:T(8,128)(2,1)S(1)}, u32[]{:S(2)}, u32[]{:S(2)}) %collective-permute-start) | collective-permute-done | bytes 524320 | tf_op jit(solution)/shard_map/ppermute | solution.py:25
  26.6 4.4 collective-permute-start.4
  31.0 19.4 %collective-permute-done.1 = bf16[1024,256]{1,0:T(8,128)(2,1)S(1)} collective-permute-done((bf16[1024,256]{1,0:T(8,128)(2,1)S(1)}, bf16[1024,256]{1,0:T(8,128)(2,1)S(1)}, u32[]{:S(2)}, u32[]{:S(2)}) %collective-permute-start.1) | collective-permute-done | bytes 524320 | tf_op jit(solution)/shard_map/ppermute | solution.py:25
  55.9 25.9 %collective-permute-done.2 = bf16[1024,256]{1,0:T(8,128)(2,1)S(1)} collective-permute-done((bf16[1024,256]{1,0:T(8,128)(2,1)S(1)}, bf16[1024,256]{1,0:T(8,128)(2,1)S(1)}, u32[]{:S(2)}, u32[]{:S(2)}) %collective-permute-start.2) | collective-permute-done | bytes 524320 | tf_op jit(solution)/shard_map/ppermute | solution.py:25
  90.0 27.2 %collective-permute-done.3 = bf16[1024,256]{1,0:T(8,128)(2,1)S(1)} collective-permute-done((bf16[1024,256]{1,0:T(8,128)(2,1)S(1)}, bf16[1024,256]{1,0:T(8,128)(2,1)S(1)}, u32[]{:S(2)}, u32[]{:S(2)}) %collective-permute-start.3) | collective-permute-done | bytes 524320 | tf_op jit(solution)/shard_map/ppermute | solution.py:25
  124.0 5.1 gather_fusion
  129.1 4.9 copy.120
  140.1 46.3 %reduce-scatter.5.cloned.1.call-done = bf16[256,1024]{1,0:T(8,128)(2,1)} async-done(((bf16[256,2048]{1,0:T(8,128)(2,1)}), bf16[256,1024]{1,0:T(8,128)(2,1)}) %reduce-scatter.5.cloned.1.call-update) | async-done | bytes 524304 | tf_op jit(solution)/shard_map/reduce_scatter | solution.py:180
  190.0 21.4 %all-gather.9.cloned.1.call-done = bf16[256,2048]{1,0:T(8,128)(2,1)} async-done(((bf16[256,1024]{1,0:T(8,128)(2,1)}), bf16[256,2048]{1,0:T(8,128)(2,1)}) %all-gather.9.cloned.1.call-update) | async-done | bytes 1048592 | tf_op jit(solution)/shard_map/all_gather | solution.py:188
  219.2 31.5 %conditional.4 = (bf16[256,2048]{1,0:T(8,128)(2,1)}, bf16[384,1024]{0,1:T(8,128)(2,1)}, bf16[384,1024]{0,1:T(8,128)(2,1)}) conditional(s32[]{:T(128)} %convert_element_type.214, () %tuple.46, (s32[2,2]{1,0:T(2,128)S(1)}, s32[]{:T(128)}, s32[2,2]{1,0:T(2,128)S(1)}, s32[2,2]{1,0:T(2,128)S(1)}, bf16[1,512,1024]{2,1,0:T(8,128)(2,1)}, ...), branch_computations={%region_7.8_spmd, %region_8.13_spmd} | conditional | flops 3363606528 | bytes 75467568 | solution.py:174
  222.7 3.5 constant_dynamic-slice_fusion.6
  230.7 3.4 fusion.96
  234.1 4.6 convolution_convert_fusion.3
  250.8 20.4 %reduce-scatter.7.cloned.1.call-done = bf16[256,1024]{1,0:T(8,128)(2,1)} async-done(((bf16[256,2048]{1,0:T(8,128)(2,1)}), bf16[256,1024]{1,0:T(8,128)(2,1)}) %reduce-scatter.7.cloned.1.call-update) | async-done | bytes 524304 | tf_op jit(solution)/shard_map/reduce_scatter | solution.py:180
  275.3 20.1 %all-gather.11.cloned.1.call-done = bf16[256,2048]{1,0:T(8,128)(2,1)} async-done(((bf16[256,1024]{1,0:T(8,128)(2,1)}), bf16[256,2048]{1,0:T(8,128)(2,1)}) %all-gather.11.cloned.1.call-update) | async-done | bytes 1048592 | tf_op jit(solution)/shard_map/all_gather | solution.py:188
  308.2 22.9 %conditional.5 = (bf16[256,2048]{1,0:T(8,128)(2,1)}, bf16[384,1024]{0,1:T(8,128)(2,1)}, bf16[384,1024]{0,1:T(8,128)(2,1)}) conditional(s32[]{:T(128)} %convert_element_type.219, () %tuple.48, (s32[2,2]{1,0:T(2,128)S(1)}, s32[]{:T(128)}, s32[2,2]{1,0:T(2,128)S(1)}, s32[2,2]{1,0:T(2,128)S(1)}, bf16[1,512,1024]{2,1,0:T(8,128)(2,1)}, ...), branch_computations={%region_14.15_spmd, %region_15.20_spmd} | conditional | flops 3363606528 | bytes 85953360 | solution.py:174
  318.2 3.5 convolution_convert_fusion.5
  331.1 3.5 select_dynamic-update-slice_fusion
  334.6 37.7 %all-gather.17.cloned.1.call-done = bf16[1,1024,2048]{2,1,0:T(8,128)(2,1)} async-done(((bf16[1,1024,256]{2,1,0:T(8,128)(2,1)}), bf16[1,1024,2048]{2,1,0:T(8,128)(2,1)}) %all-gather.17.cloned.1.call-update) | async-done | bytes 4194320 | tf_op jit(solution)/shard_map/all_gather | solution.py:145
  372.3 8.8 %fusion.51 = f32[768,2048]{1,0:T(8,128)} fusion(bf16[768,1024]{0,1:T(8,128)(2,1)} %get-tuple-element.478, bf16[1,1024,2048]{2,1,0:T(8,128)(2,1)} %all-gather.17.cloned.1.call-done), kind=kOutput, calls=%fused_computation.107 | convolution fusion | flops 3221225472 | bytes 12058624 | tf_op jit(solution)/shard_map/dot_general | solution.py:206
  381.1 66.5 %all-gather.15.cloned.1.call-done = bf16[1,1024,2048]{2,1,0:T(8,128)(2,1)} async-done(((bf16[1,1024,256]{2,1,0:T(8,128)(2,1)}), bf16[1,1024,2048]{2,1,0:T(8,128)(2,1)}) %all-gather.15.cloned.1.call-update) | async-done | bytes 4194320 | tf_op jit(solution)/shard_map/all_gather | solution.py:144
  447.6 9.6 %add_convert_fusion = bf16[768,2048]{1,0:T(8,128)(2,1)} fusion(f32[768,2048]{1,0:T(8,128)} %fusion.51, bf16[768,1024]{0,1:T(8,128)(2,1)} %get-tuple-element.479, bf16[1,1024,2048]{2,1,0:T(8,128)(2,1)} %all-gather.15.cloned.1.call-done), kind=kOutput, calls=%fused_computation.106 | convolution fusion | flops 3224371200 | bytes 15204352 | tf_op jit(solution)/shard_map/dot_general | solution.py:206
  459.4 34.2 %reduce-scatter.11.cloned.1.call-done = bf16[768,512]{1,0:T(8,128)(2,1)} async-done(((bf16[768,2048]{1,0:T(8,128)(2,1)}), bf16[768,512]{1,0:T(8,128)(2,1)}) %reduce-scatter.11.cloned.1.call-update) | async-done | bytes 786448 | tf_op jit(solution)/shard_map/reduce_scatter | solution.py:209
  502.7 13.5 %reduce-scatter.9.cloned.1.call-done = bf16[256,1024]{1,0:T(8,128)(2,1)} async-done(((bf16[256,2048]{1,0:T(8,128)(2,1)}), bf16[256,1024]{1,0:T(8,128)(2,1)}) %reduce-scatter.9.cloned.1.call-update) | async-done | bytes 524304 | tf_op jit(solution)/shard_map/reduce_scatter | solution.py:180
  (181 shorter events, 117.5 us)
Async XLA Ops:
  7.2 129.8 %all-gather.13.cloned.1.call-start = ((), (), s32[]{:S(2)}) async-start(), calls=%async_computation.10 | async-start | bytes 4718592 | tf_op jit(solution)/shard_map/all_gather | solution.py:142
  7.9 178.5 %reduce-scatter.5.cloned.1.call-start = ((), (), s32[]{:S(2)}) async-start(), calls=%async_computation.4 | async-start | bytes 1572864 | tf_op jit(solution)/shard_map/reduce_scatter | solution.py:180
  7.9 18.4 %collective-permute-start = (bf16[1024,256]{1,0:T(8,128)(2,1)}, bf16[1024,256]{1,0:T(8,128)(2,1)S(1)}, u32[]{:S(2)}, u32[]{:S(2)}) collective-permute-start(bf16[1024,256]{1,0:T(8,128)(2,1)} %bitcast.254), channel_id=1, source_target_pairs={{0,2},{2,4},{4,6},{6,8},{8,10},{10,12},{12,14},{14,0},{1,3},{3,5},... | collective-permute-start | bytes 1572872 | tf_op jit(solution)/shard_map/ppermute | solution.py:25
  26.3 24.1 %collective-permute-start.1 = (bf16[1024,256]{1,0:T(8,128)(2,1)S(1)}, bf16[1024,256]{1,0:T(8,128)(2,1)S(1)}, u32[]{:S(2)}, u32[]{:S(2)}) collective-permute-start(bf16[1024,256]{1,0:T(8,128)(2,1)S(1)} %collective-permute-done), channel_id=1, source_target_pairs={{0,2},{2,4},{4,6},{6,8},{8,10},{10,12},{12,14},{14,0},{1,3},{3,5},... | collective-permute-start | bytes 1572872 | tf_op jit(solution)/shard_map/ppermute | solution.py:25
  26.6 27.6 %collective-permute-start.4 = (bf16[1024,256]{1,0:T(8,128)(2,1)}, bf16[1024,256]{1,0:T(8,128)(2,1)S(1)}, u32[]{:S(2)}, u32[]{:S(2)}) collective-permute-start(bf16[1024,256]{1,0:T(8,128)(2,1)} %bitcast.255), channel_id=1, source_target_pairs={{2,0},{4,2},{6,4},{8,6},{10,8},{12,10},{14,12},{0,14},{3,1},{5,3},... | collective-permute-start | bytes 1572872 | tf_op jit(solution)/shard_map/ppermute | solution.py:27
  50.4 31.5 %collective-permute-start.2 = (bf16[1024,256]{1,0:T(8,128)(2,1)S(1)}, bf16[1024,256]{1,0:T(8,128)(2,1)S(1)}, u32[]{:S(2)}, u32[]{:S(2)}) collective-permute-start(bf16[1024,256]{1,0:T(8,128)(2,1)S(1)} %collective-permute-done.1), channel_id=1, source_target_pairs={{0,2},{2,4},{4,6},{6,8},{8,10},{10,12},{12,14},{14,0},{1,3},{3,5},... | collective-permute-start | bytes 1572872 | tf_op jit(solution)/shard_map/ppermute | solution.py:25
  54.2 32.7 %collective-permute-start.5 = (bf16[1024,256]{1,0:T(8,128)(2,1)S(1)}, bf16[1024,256]{1,0:T(8,128)(2,1)S(1)}, u32[]{:S(2)}, u32[]{:S(2)}) collective-permute-start(bf16[1024,256]{1,0:T(8,128)(2,1)S(1)} %collective-permute-done.4), channel_id=1, source_target_pairs={{2,0},{4,2},{6,4},{8,6},{10,8},{12,10},{14,12},{0,14},{3,1},{5,3},... | collective-permute-start | bytes 1572872 | tf_op jit(solution)/shard_map/ppermute | solution.py:27
  81.9 35.4 %collective-permute-start.3 = (bf16[1024,256]{1,0:T(8,128)(2,1)S(1)}, bf16[1024,256]{1,0:T(8,128)(2,1)S(1)}, u32[]{:S(2)}, u32[]{:S(2)}) collective-permute-start(bf16[1024,256]{1,0:T(8,128)(2,1)S(1)} %collective-permute-done.2), channel_id=1, source_target_pairs={{0,2},{2,4},{4,6},{6,8},{8,10},{10,12},{12,14},{14,0},{1,3},{3,5},... | collective-permute-start | bytes 1572872 | tf_op jit(solution)/shard_map/ppermute | solution.py:25
  86.9 36.2 %collective-permute-start.6 = (bf16[1024,256]{1,0:T(8,128)(2,1)S(1)}, bf16[1024,256]{1,0:T(8,128)(2,1)S(1)}, u32[]{:S(2)}, u32[]{:S(2)}) collective-permute-start(bf16[1024,256]{1,0:T(8,128)(2,1)S(1)} %collective-permute-done.5), channel_id=1, source_target_pairs={{2,0},{4,2},{6,4},{8,6},{10,8},{12,10},{14,12},{0,14},{3,1},{5,3},... | collective-permute-start | bytes 1572872 | tf_op jit(solution)/shard_map/ppermute | solution.py:27
  129.0 7.9 %copy-start.24 = (s32[2,2]{1,0:T(2,128)S(1)}, s32[2,2]{1,0:T(2,128)}, u32[]{:S(2)}) copy-start(s32[2,2]{1,0:T(2,128)} %param.27) | copy-start | bytes 52
  129.0 7.9 %copy-start.25 = (s32[2,2]{1,0:T(2,128)S(1)}, s32[2,2]{1,0:T(2,128)}, u32[]{:S(2)}) copy-start(s32[2,2]{1,0:T(2,128)} %param.28) | copy-start | bytes 52
  140.0 71.4 %all-gather.9.cloned.1.call-start = ((), (), s32[]{:S(2)}) async-start(), calls=%async_computation.5 | async-start | bytes 1572864 | tf_op jit(solution)/shard_map/all_gather | solution.py:188
  189.9 81.3 %reduce-scatter.7.cloned.1.call-start = ((), (), s32[]{:S(2)}) async-start(), calls=%async_computation.6 | async-start | bytes 1572864 | tf_op jit(solution)/shard_map/reduce_scatter | solution.py:180
  211.4 4.9 collective-permute-start.7
  250.8 44.6 %all-gather.11.cloned.1.call-start = ((), (), s32[]{:S(2)}) async-start(), calls=%async_computation.7 | async-start | bytes 1572864 | tf_op jit(solution)/shard_map/all_gather | solution.py:188
  273.9 98.4 %all-gather.17.cloned.1.call-start = ((), (), s32[]{:S(2)}) async-start(), calls=%async_computation.12 | async-start | bytes 4718592 | tf_op jit(solution)/shard_map/all_gather | solution.py:145
  274.5 173.1 %all-gather.15.cloned.1.call-start = ((), (), s32[]{:S(2)}) async-start(), calls=%async_computation.11 | async-start | bytes 4718592 | tf_op jit(solution)/shard_map/all_gather | solution.py:144
  275.2 218.3 %reduce-scatter.11.cloned.1.call-start = ((), (), s32[]{:S(2)}) async-start(), calls=%async_computation.9 | async-start | bytes 3932160 | tf_op jit(solution)/shard_map/reduce_scatter | solution.py:209
  295.4 11.4 %collective-permute-start.8 = (bf16[256,2048]{1,0:T(8,128)(2,1)}, bf16[256,2048]{1,0:T(8,128)(2,1)S(1)}, u32[]{:S(2)}, u32[]{:S(2)}) collective-permute-start(bf16[256,2048]{1,0:T(8,128)(2,1)} %all-gather.11.cloned.1.call-done), channel_id=1, source_target_pairs={{16,0},{17,1},{18,2},{19,3},{20,4},{21,5},{22,6},{23,7},{24,8},{25... | collective-permute-start | bytes 3145736 | tf_op jit(solution)/shard_map/ppermute | solution.py:37
  457.3 59.0 %reduce-scatter.9.cloned.1.call-start = ((), (), s32[]{:S(2)}) async-start(), calls=%async_computation.8 | async-start | bytes 1572864 | tf_op jit(solution)/shard_map/reduce_scatter | solution.py:180
  495.7 20.6 %copy-start.12 = (bf16[256,2048]{1,0:T(8,128)(2,1)S(1)}, bf16[256,2048]{1,0:T(8,128)(2,1)}, u32[]{:S(2)}) copy-start(bf16[256,2048]{1,0:T(8,128)(2,1)} %dynamic-slice_select_fusion) | copy-start | bytes 3145732
  495.7 22.5 %collective-permute-start.9 = (bf16[256,512]{1,0:T(8,128)(2,1)S(1)}, bf16[256,512]{1,0:T(8,128)(2,1)S(1)}, u32[]{:S(2)}, u32[]{:S(2)}) collective-permute-start(bf16[256,512]{1,0:T(8,128)(2,1)S(1)} %bitcast.268), channel_id=1, source_target_pairs={{0,2},{2,4},{4,6},{6,8},{8,10},{10,12},{12,14},{14,0},{1,3},{3,5},... | collective-permute-start | bytes 786440 | tf_op jit(solution)/shard_map/ppermute | solution.py:46
  498.0 20.5 %collective-permute-start.10 = (bf16[256,512]{1,0:T(8,128)(2,1)}, bf16[256,512]{1,0:T(8,128)(2,1)}, u32[]{:S(2)}, u32[]{:S(2)}) collective-permute-start(bf16[256,512]{1,0:T(8,128)(2,1)} %bitcast.79), channel_id=1, source_target_pairs={{2,0},{4,2},{6,4},{8,6},{10,8},{12,10},{14,12},{0,14},{3,1},{5,3},... | collective-permute-start | bytes 786440 | tf_op jit(solution)/shard_map/ppermute | solution.py:49
  502.7 15.0 %copy-start.4 = (bf16[768,512]{1,0:T(8,128)(2,1)S(1)}, bf16[768,512]{1,0:T(8,128)(2,1)}, u32[]{:S(2)}) copy-start(bf16[768,512]{1,0:T(8,128)(2,1)} %reduce-scatter.11.cloned.1.call-done) | copy-start | bytes 2359300
  (20 other events, 61.4 us)
Sparse Core Ops, SparseCore 0:
  10.0 126.8 all-gather.12
  140.1 46.2 reduce-scatter.4
  190.0 21.2 all-gather.8
  250.9 20.3 reduce-scatter.6
  274.0 21.2 all-gather.10
  297.3 75.0 all-gather.16
  374.4 73.1 all-gather.14
  457.4 36.1 reduce-scatter.10
  495.9 20.3 reduce-scatter.8
